TPU v7x, 32 devices: a whole 2x2x4 slice. The times are simulated.
32 devices in a mesh: parts: 2 (over x), sta: 16 (over z, y, core).
Axes of the slice: x: 2, y: 2, z: 4, core: 2. Of those that a mesh axis runs over, the one named last changes fastest.
Arguments:
- data: bfloat16 [32, 3, 896], P(('parts', 'sta')), parts along dimension 0, may hold values from -40 to 40
- templates: bfloat16 [128, 3, 512], P('sta'), may hold values from -12 to 12
- station_lists: int32 [16, 128], replicated, may hold values from 0 to 15, as said below
- counts: int32 [128], replicated, may hold values from 8 to 16
- offsets: int32 [16, 128], replicated, may hold values from 0 to 127
Outputs:
- detection: float32 [256, 256], P(('parts', 'sta')), parts along dimension 0
There are 2 independent parts, one for each index of `parts`. A program takes and returns all parts, laid end to end along the dimension named above; an argument that names none is the same for every part. Nothing has to cross between parts.
Inputs may be any that keep to these rules, and one draw needn't show every extreme that they name: `station_lists`: each column names every one of the 16 stations once; template t uses the stations in entries k < counts[t] of its column. offsets[k, t] belongs to the station in entry k of template t's column.
All inputs are finite; a program needn't handle non-finite values.
Results may differ from a plain program's by a relative error of at most 0.0028.
Values may be sent and summed in bfloat16 or wider, within the bound.
A program may use at most 64 MiB of HBM per device.

v0:
```python
import math
import jax
import jax.numpy as jnp
from jax import lax
from jax.sharding import PartitionSpec as P

NCH = 3
L = 512
NTAU = 256


def center_templates(templates):
    values = templates.astype(jnp.float32)
    return (values - jnp.mean(values, axis=2, keepdims=True)).astype(jnp.bfloat16)


def template_scale(centered):
    values = centered.astype(jnp.float32)
    return jnp.sqrt(jnp.mean(values * values, axis=2) + 1e-06)


def sample_blocks(samples, lag_count):
    item_count, channel_count, length = samples.shape
    width = length - lag_count
    block_count = lag_count // 128
    reshaped = samples.reshape(item_count, channel_count, length // 128, 128)
    return jnp.concatenate(
        [
            reshaped[:, :, step_index : step_index + block_count]
            for step_index in range(width // 128 + 1)
        ],
        axis=3,
    )


def window_scale(blocks, width):
    block_span = blocks.shape[3]
    column = lax.broadcasted_iota(jnp.int32, (block_span, 128), 0)
    lane_index = lax.broadcasted_iota(jnp.int32, (block_span, 128), 1)
    window = ((column >= lane_index) & (column < lane_index + width)).astype(jnp.float32)
    values = blocks.astype(jnp.float32)
    window_sum = jnp.einsum("scbj,jr->scbr", values, window, precision=lax.Precision.HIGHEST)
    square_sum = jnp.einsum(
        "scbj,jr->scbr", values * values, window, precision=lax.Precision.HIGHEST
    )
    out_shape = (blocks.shape[0], blocks.shape[1], blocks.shape[2] * 128)
    mean_one = window_sum.reshape(out_shape) / width
    mean_two = square_sum.reshape(out_shape) / width
    return jnp.sqrt(mean_two - mean_one * mean_one + 1e-05)


def link_tables(station_lists, counts, offsets, width):
    listed = station_lists.shape[0]
    wanted = lax.broadcasted_iota(jnp.int32, (1, 1, width), 2)
    in_count = lax.broadcasted_iota(jnp.int32, (listed, 1, 1), 0) < counts[None, :, None]
    matches = (station_lists[:, :, None] == wanted) & in_count
    member = jnp.any(matches, axis=0).astype(jnp.float32)
    shifts = jnp.sum(jnp.where(matches, offsets[:, :, None], 0), axis=0)
    return (member, shifts)


def stack_rows(fitted, member, shifts, lags_out):
    current = fitted
    bit_count = (fitted.shape[2] - lags_out - 1).bit_length()
    for bit_number in reversed(range(bit_count)):
        shift_step = 1 << bit_number
        kept_width = current.shape[2] - shift_step
        chosen = shifts >> bit_number & 1 == 1
        current = jnp.where(
            chosen[:, :, None], current[:, :, shift_step:], current[:, :, :kept_width]
        )
    return jnp.sum(member[:, :, None] * current[:, :, :lags_out], axis=1)


def body(data, templates, station_lists, counts, offsets):
    lag_count = data.shape[2] - L
    centered = center_templates(templates)
    own_templates = templates.shape[0]
    own_first = lax.axis_index("sta") * own_templates
    own_lists = lax.dynamic_slice_in_dim(station_lists, own_first, own_templates, 1)
    own_counts = lax.dynamic_slice_in_dim(counts, own_first, own_templates, 0)
    own_offsets = lax.dynamic_slice_in_dim(offsets, own_first, own_templates, 1)
    samples_all = lax.all_gather(data, "sta", axis=0, tiled=True)
    station_total = samples_all.shape[0]
    member, shifts = link_tables(own_lists, own_counts, own_offsets, station_total)
    chan_norms = template_scale(centered)
    block_span = L + 128
    padded = jnp.pad(centered, ((0, 0), (0, 0), (0, 129)))
    repeated = jnp.tile(padded, (1, 1, 128))
    toeplitz = repeated[:, :, : 128 * block_span].reshape(own_templates, NCH, 128, block_span)
    toeplitz = jnp.transpose(toeplitz, (1, 3, 0, 2)).reshape(NCH, block_span, own_templates * 128)
    group_size = math.gcd(station_total, 64)

    def add_stations(step_index, running):
        blocks = sample_blocks(samples_all, lag_count)
        scales = window_scale(blocks, L)
        block_count = blocks.shape[2]
        products = jnp.einsum(
            "scbj,cjq->scbq", blocks, toeplitz, preferred_element_type=jnp.float32
        )
        products = products.reshape(group_size, NCH, block_count, own_templates, 128)
        products = jnp.transpose(products, (3, 0, 1, 2, 4)).reshape(
            own_templates, group_size, NCH, block_count * 128
        )
        normalized = products / (L * chan_norms[:, None, :, None] * scales[None])
        fitted = jnp.sum(normalized, axis=2) / NCH
        return running + stack_rows(fitted, member, shifts, NTAU)

    zero_rows = jnp.zeros((own_templates, NTAU), jnp.float32)
    return lax.fori_loop(0, station_total // group_size, add_stations, zero_rows)


def solution(mesh):
    placed = (P(("parts", "sta"), None, None), P("sta", None, None), P(), P(), P())
    return jax.shard_map(
        body, mesh=mesh, in_specs=placed, out_specs=P(("parts", "sta"), None), check_vma=False
    )
```

profile of v0, /device:TPU:0, one launch (start us, length us, event | category | flops | bytes accessed | tf_op | source)
XLA Modules:
  0.0 48.1 jit_solution(976873297776806663)
XLA Ops:
  0.0 0.8 %convert_reduce_fusion = f32[8,3]{0,1:T(4,128)S(1)} fusion(bf16[8,3,512]{2,0,1:T(8,128)(2,1)} %param.6), kind=kLoop, calls=%fused_computation.32 | loop fusion | flops 24552 | bytes 24672 | tf_op jit(solution)/shard_map/reduce_sum | solution.py:14
  0.8 0.9 %multiply_reduce_fusion = (f32[8,3]{0,1:T(4,128)S(1)}, bf16[8,3,512]{2,0,1:T(8,128)(2,1)S(1)}) fusion(f32[8,3]{0,1:T(4,128)S(1)} %broadcast_multiply_fusion.1, bf16[8,3,512]{2,0,1:T(8,128)(2,1)} %param.6), kind=kLoop, calls=%fused_computation.34 | loop fusion | flops 73704 | bytes 49344 | tf_op jit(solution)/shard_map/reduce_sum | solution.py:19
  1.7 2.4 %tile.4 = bf16[8,3,128,641]{3,2,0,1:T(8,128)(2,1)} broadcast(bf16[8,3,641]{2,0,1:T(8,128)(2,1)S(1)} %pad.4), dimensions={0,1,3} | broadcast | bytes 3969072 | tf_op jit(solution)/shard_map/tile | solution.py:89
  4.2 8.7 %tile.10 = bf16[8,3,82048]{2,0,1:T(8,128)(2,1)} reshape(bf16[8,3,128,641]{3,2,0,1:T(8,128)(2,1)} %tile.4) | data formatting | bytes 7876608 | tf_op jit(solution)/shard_map/tile | solution.py:89
  12.9 0.0 slice-start
  12.9 2.1 %slice-done = bf16[8,3,81920]{2,0,1:T(8,128)(2,1)S(1)} async-done(((bf16[8,3,82048]{2,0,1:T(8,128)(2,1)}), bf16[8,3,81920]{2,0,1:T(8,128)(2,1)S(1)}, s32[]{:S(2)}) %slice-start) | async-done | bytes 3932184 | tf_op jit(solution)/shard_map/slice | solution.py:90
  15.0 0.0 copy-start.2
  15.0 2.6 %copy.54 = bf16[3,8,128,640]{3,2,1,0:T(8,128)(2,1)} copy(bf16[3,8,128,640]{3,1,2,0:T(8,128)(2,1)S(1)} %bitcast.41) | data formatting | bytes 7864320
  17.6 0.0 copy-done.2
  17.6 23.4 %all_gather.3 = bf16[16,3,896]{2,1,0:T(4,128)(2,1)S(1)} all-gather(bf16[1,3,896]{2,1,0:T(4,128)(2,1)S(1)} %copy-done.2), channel_id=1, replica_groups=mesh['parts'=2,'sta'=16] {'sta'}, dimensions={0}, use_global_device_ids=true | all-gather | bytes 91392 | tf_op jit(solution)/shard_map/all_gather | solution.py:83
  40.9 0.1 reshape.121
  41.0 0.1 fusion.20
  41.2 0.0 copy-start
  41.2 0.0 copy-start.1
  41.3 0.0 copy-start.3
  41.3 3.4 %fusion.21 = f32[3,1024,16,3]{1,2,3,0:T(8,128)S(1)} fusion(bf16[3,640,1024,1]{1,2,3,0:T(8,128)(2,1)} %bitcast.40, bf16[16,3,3,640]{3,0,2,1:T(8,128)(2,1)S(1)} %copy_dynamic-update-slice_fusion), kind=kOutput, calls=%fused_computation.55 | convolution fusion | flops 188743680 | bytes 4706304 | tf_op jit(solution)/shard_map/while/body/eval_jaxpr/scbj,cjq->scbq/dot_general | solution.py:98
  44.7 0.1 copy.47
  44.8 0.4 convolution_multiply_fusion.1
  45.2 0.3 fusion.3
  45.5 0.2 fusion.4
  45.7 0.1 copy.29
  45.8 0.1 div.31
  45.9 0.0 copy-done
  45.9 0.0 copy-done.1
  45.9 0.1 constant_dynamic-slice_fusion
  46.0 0.0 copy-done.3
  46.0 0.1 dynamic_slice.10
  46.1 0.1 select_reduce_fusion
  46.3 0.1 slice_select_fusion.5
  46.4 0.1 slice_select_fusion.4
  46.5 0.1 slice_select_fusion.3
  46.7 0.1 slice_select_fusion.2
  46.8 0.1 slice_select_fusion.1
  47.0 0.1 slice_select_fusion
  47.1 0.1 fusion.19
  47.2 0.1 fusion.16
  47.4 0.7 %fusion.14 = f32[8,256]{1,0:T(8,128)} fusion(f32[8,16,257]{2,1,0:T(8,128)S(1)} %get-tuple-element.20, f32[8,16,257]{2,1,0:T(8,128)S(1)} %get-tuple-element.19, f32[8,16]{1,0:T(8,128)S(1)} %convert_element_type.24, pred[8,16]{1,0:T(8,128)(4,1)S(1)} %get-tuple-element.35), kind=kLoop, calls=%fused_computation.25 | loop fusion | flops 96256 | bytes 270976 | tf_op jit(solution)/shard_map/while/body/eval_jaxpr/reduce_sum | solution.py:72
  (13 shorter events, 0.1 us)
Async XLA Ops:
  12.9 2.1 %slice-start = ((bf16[8,3,82048]{2,0,1:T(8,128)(2,1)}), bf16[8,3,81920]{2,0,1:T(8,128)(2,1)S(1)}, s32[]{:S(2)}) async-start(bf16[8,3,82048]{2,0,1:T(8,128)(2,1)} %tile.10), calls=%async_computation | async-start | bytes 7864320 | tf_op jit(solution)/shard_map/slice | solution.py:90
  15.0 2.6 %copy-start.2 = (bf16[1,3,896]{2,1,0:T(4,128)(2,1)S(1)}, bf16[1,3,896]{2,1,0:T(4,128)(2,1)}, u32[]{:S(2)}) copy-start(bf16[1,3,896]{2,1,0:T(4,128)(2,1)} %param.5) | copy-start | bytes 16132
  41.2 4.7 %copy-start = (s32[16,128]{1,0:T(8,128)S(1)}, s32[16,128]{1,0:T(8,128)}, u32[]{:S(2)}) copy-start(s32[16,128]{1,0:T(8,128)} %param.9) | copy-start | bytes 24580
  41.2 4.7 %copy-start.1 = (s32[16,128]{1,0:T(8,128)S(1)}, s32[16,128]{1,0:T(8,128)}, u32[]{:S(2)}) copy-start(s32[16,128]{1,0:T(8,128)} %param.7) | copy-start | bytes 24580
  41.3 4.8 %copy-start.3 = (s32[128]{0:T(128)S(1)}, s32[128]{0:T(128)}, u32[]{:S(2)}) copy-start(s32[128]{0:T(128)} %param.8) | copy-start | bytes 1540
where the time goes:
time: 48.4 us; the launch traced here: 48.1 us
  blocking collectives  23.4 us (48%)
  local copies, waits for them, and re-layouts  16.7 us (35%)
  matrix products  4.02 us (8%)
  other arithmetic  3.7 us (8%)
    all_gather x1, blocking collectives, body(): samples_all = lax.all_gather(data, 'sta', axis=0, tiled=True)  23.4 us
    another operation x2, local copies, waits for them, and re-layouts, body(): repeated = jnp.tile(padded, (1, 1, 128))  11.2 us
    dot_general x1, matrix products, add_stations(): jnp.einsum('scbj,cjq->scbq', blocks, toeplitz, preferred_element_type=jnp...  3.4 us
    unnamed x14, local copies, waits for them, and re-layouts  2.75 us
    slice x2, local copies, waits for them, and re-layouts, body(): repeated[:, :, :128 * block_span]  2.11 us

commit v1 on v0

--- a/solution.py
+++ b/solution.py
@@ -80,7 +80,14 @@
     own_lists = lax.dynamic_slice_in_dim(station_lists, own_first, own_templates, 1)
     own_counts = lax.dynamic_slice_in_dim(counts, own_first, own_templates, 0)
     own_offsets = lax.dynamic_slice_in_dim(offsets, own_first, own_templates, 1)
-    samples_all = lax.all_gather(data, "sta", axis=0, tiled=True)
+    ways, here, step = (lax.axis_size("sta"), lax.axis_index("sta"), data.shape[0])
+    line, have = (data, 1)
+    while have < ways:
+        line = jnp.concatenate(
+            [line, lax.ppermute(line, "sta", [(d, (d - have) % ways) for d in range(ways)])], axis=0
+        )
+        have = 2 * have
+    samples_all = jnp.roll(line, here * step, axis=0)
     station_total = samples_all.shape[0]
     member, shifts = link_tables(own_lists, own_counts, own_offsets, station_total)
     chan_norms = template_scale(centered)

time: 48.4 us -> 45.8 us (0.946)
  blocking collectives: 23.4 us -> 0 us
  waiting for transfers between devices: 0 us -> 11.7 us
  starting transfers between devices: 0 us -> 6.63 us
  local copies, waits for them, and re-layouts: 16.7 us -> 19 us
    all_gather x1 -> x0, blocking collectives: 23.4 us -> none  [body(): samples_all = lax.all_gather(data, 'sta', axis=0, tiled=True)]
    ppermute x0 -> x4, waiting for transfers between devices: none -> 11.7 us  [body(): lax.ppermute(line, 'sta', [(d, (d - have) % ways) for d in range(ways)])]
    ppermute x0 -> x4, starting transfers between devices: none -> 6.63 us  [body(): lax.ppermute(line, 'sta', [(d, (d - have) % ways) for d in range(ways)])]
    unnamed x14 -> x17, local copies, waits for them, and re-layouts: 2.75 us -> 3.6 us
    dynamic_slice x1, local copies, waits for them, and re-layouts: 0.08 us -> 0.79 us  [body(): own_offsets = lax.dynamic_slice_in_dim(offsets, own_first, own_templates, 1)]
    dynamic_slice x1, local copies, waits for them, and re-layouts: 0.07 us -> 0.73 us  [body(): own_counts = lax.dynamic_slice_in_dim(counts, own_first, own_templates, 0)]
  transfers between devices with their start and end apart: 0 -> 4, of which waited for: 0 -> 3; matrix products, arithmetic and copies ran while one was open for 0% -> 40% of each run, Pallas kernels for 0% -> 0%
where the time goes in v1:
time: 45.8 us; the launch traced here: 45.5 us
  local copies, waits for them, and re-layouts  19 us (41%)
  waiting for transfers between devices  11.7 us (26%)
  starting transfers between devices  6.63 us (14%)
  matrix products  4 us (9%)
  other arithmetic  3.79 us (8%)
    ppermute x4, waiting for transfers between devices, body(): lax.ppermute(line, 'sta', [(d, (d - have) % ways) for d in range(ways)])  11.7 us
    another operation x2, local copies, waits for them, and re-layouts, body(): repeated = jnp.tile(padded, (1, 1, 128))  11.1 us
    ppermute x4, starting transfers between devices, body(): lax.ppermute(line, 'sta', [(d, (d - have) % ways) for d in range(ways)])  6.63 us
    unnamed x17, local copies, waits for them, and re-layouts  3.6 us
    dot_general x1, matrix products, add_stations(): jnp.einsum('scbj,cjq->scbq', blocks, toeplitz, preferred_element_type=jnp...  3.39 us
    slice x2, local copies, waits for them, and re-layouts, body(): repeated[:, :, :128 * block_span]  2.11 us
  transfers between devices with their start and end apart: 4, of which 3 were waited for; matrix products, arithmetic and copies ran while one was open for 40% of the time, Pallas kernels for 0%

profile of v1, /device:TPU:0, one launch (start us, length us, event | category | flops | bytes accessed | tf_op | source)
XLA Modules:
  0.0 45.5 jit_solution(5987763696525798213)
XLA Ops:
  0.0 5.4 %collective-permute-start = (bf16[1,3,896]{2,1,0:T(4,128)(2,1)}, bf16[1,3,896]{2,1,0:T(4,128)(2,1)S(1)}, u32[]{:S(2)}, u32[]{:S(2)}) collective-permute-start(bf16[1,3,896]{2,1,0:T(4,128)(2,1)} %param.5), channel_id=1, source_target_pairs={{0,15},{1,0},{2,1},{3,2},{4,3},{5,4},{6,5},{7,6},{8,7},{9,8},{10,9... | collective-permute-start | bytes 16136 | tf_op jit(solution)/shard_map/ppermute | solution.py:87
  5.4 0.7 %constant_dynamic-update-slice_fusion.9 = bf16[32,3,896]{2,1,0:T(4,128)(2,1)S(1)} fusion(bf16[1,3,896]{2,1,0:T(4,128)(2,1)} %param.5), kind=kLoop, calls=%fused_computation.50 | loop fusion | bytes 12544
  6.2 0.8 %convert_reduce_fusion = f32[8,3]{0,1:T(4,128)S(1)} fusion(bf16[8,3,512]{2,0,1:T(8,128)(2,1)} %param.6), kind=kLoop, calls=%fused_computation.32 | loop fusion | flops 24552 | bytes 24672 | tf_op jit(solution)/shard_map/reduce_sum | solution.py:14
  7.0 0.9 %multiply_reduce_fusion = (f32[8,3]{0,1:T(4,128)S(1)}, bf16[8,3,512]{2,0,1:T(8,128)(2,1)S(1)}) fusion(f32[8,3]{0,1:T(4,128)S(1)} %broadcast_multiply_fusion.1, bf16[8,3,512]{2,0,1:T(8,128)(2,1)} %param.6), kind=kLoop, calls=%fused_computation.35 | loop fusion | flops 73704 | bytes 49344 | tf_op jit(solution)/shard_map/reduce_sum | solution.py:19
  7.9 0.7 %dynamic_slice.14 = s32[8]{0:T(128)S(1)} dynamic-slice(s32[128]{0:T(128)} %param.8, s32[]{:T(128)S(6)} %select_n.57), dynamic_slice_sizes={8} | dynamic-slice | bytes 68 | tf_op jit(solution)/shard_map/dynamic_slice | solution.py:81
  8.7 0.8 %constant_dynamic-slice_fusion.1 = (s32[16,8]{1,0:T(8,128)S(1)}, s32[16,8]{1,0:T(8,128)S(1)}) fusion(s32[16,128]{1,0:T(8,128)} %param.9, s32[]{:T(128)S(6)} %select_n.57, s32[16,128]{1,0:T(8,128)} %param.7), kind=kLoop, calls=%fused_computation.64 | loop fusion | bytes 2052 | tf_op jit(solution)/shard_map/dynamic_slice | solution.py:82
  9.4 0.1 fusion.16
  9.6 0.1 select_reduce_fusion
  9.7 2.4 %tile.4 = bf16[8,3,128,641]{3,2,0,1:T(8,128)(2,1)} broadcast(bf16[8,3,641]{2,0,1:T(8,128)(2,1)S(1)} %pad.4), dimensions={0,1,3} | broadcast | bytes 3969072 | tf_op jit(solution)/shard_map/tile | solution.py:96
  12.2 8.7 %tile.10 = bf16[8,3,82048]{2,0,1:T(8,128)(2,1)} reshape(bf16[8,3,128,641]{3,2,0,1:T(8,128)(2,1)} %tile.4) | data formatting | bytes 7876608 | tf_op jit(solution)/shard_map/tile | solution.py:96
  20.9 0.0 slice-start
  20.9 2.1 %slice-done = bf16[8,3,81920]{2,0,1:T(8,128)(2,1)S(1)} async-done(((bf16[8,3,82048]{2,0,1:T(8,128)(2,1)}), bf16[8,3,81920]{2,0,1:T(8,128)(2,1)S(1)}, s32[]{:S(2)}) %slice-start) | async-done | bytes 3932184 | tf_op jit(solution)/shard_map/slice | solution.py:97
  23.0 0.0 copy-start
  23.0 2.6 %copy.54 = bf16[3,8,128,640]{3,2,1,0:T(8,128)(2,1)} copy(bf16[3,8,128,640]{3,1,2,0:T(8,128)(2,1)S(1)} %bitcast.41) | data formatting | bytes 7864320
  25.6 0.0 collective-permute-done
  25.6 0.0 copy-done
  25.6 0.6 %collective-permute-start.1 = (bf16[2,3,896]{2,1,0:T(4,128)(2,1)S(1)}, bf16[2,3,896]{2,1,0:T(4,128)(2,1)S(1)}, u32[]{:S(2)}, u32[]{:S(2)}) collective-permute-start(bf16[2,3,896]{2,1,0:T(4,128)(2,1)S(1)} %pad_maximum_fusion.2), channel_id=1, source_target_pairs={{0,14},{1,15},{2,0},{3,1},{4,2},{5,3},{6,4},{7,5},{8,6},{9,7},{10,... | collective-permute-start | bytes 32264 | tf_op jit(solution)/shard_map/ppermute | solution.py:87
  26.2 3.1 %collective-permute-done.1 = bf16[2,3,896]{2,1,0:T(4,128)(2,1)S(1)} collective-permute-done((bf16[2,3,896]{2,1,0:T(4,128)(2,1)S(1)}, bf16[2,3,896]{2,1,0:T(4,128)(2,1)S(1)}, u32[]{:S(2)}, u32[]{:S(2)}) %collective-permute-start.1) | collective-permute-done | bytes 10784 | tf_op jit(solution)/shard_map/ppermute | solution.py:87
  29.4 0.5 %collective-permute-start.2 = (bf16[4,3,896]{2,1,0:T(4,128)(2,1)S(1)}, bf16[4,3,896]{2,1,0:T(4,128)(2,1)S(1)}, u32[]{:S(2)}, u32[]{:S(2)}) collective-permute-start(bf16[4,3,896]{2,1,0:T(4,128)(2,1)S(1)} %pad_maximum_fusion.1), channel_id=1, source_target_pairs={{0,12},{1,13},{2,14},{3,15},{4,0},{5,1},{6,2},{7,3},{8,4},{9,5},{1... | collective-permute-start | bytes 64520 | tf_op jit(solution)/shard_map/ppermute | solution.py:87
  29.9 3.4 %collective-permute-done.2 = bf16[4,3,896]{2,1,0:T(4,128)(2,1)S(1)} collective-permute-done((bf16[4,3,896]{2,1,0:T(4,128)(2,1)S(1)}, bf16[4,3,896]{2,1,0:T(4,128)(2,1)S(1)}, u32[]{:S(2)}, u32[]{:S(2)}) %collective-permute-start.2) | collective-permute-done | bytes 21536 | tf_op jit(solution)/shard_map/ppermute | solution.py:87
  33.4 0.1 collective-permute-start.3
  33.5 5.2 %collective-permute-done.3 = bf16[8,3,896]{2,1,0:T(4,128)(2,1)S(1)} collective-permute-done((bf16[8,3,896]{2,1,0:T(4,128)(2,1)S(1)}, bf16[8,3,896]{2,1,0:T(4,128)(2,1)S(1)}, u32[]{:S(2)}, u32[]{:S(2)}) %collective-permute-start.3) | collective-permute-done | bytes 43040 | tf_op jit(solution)/shard_map/ppermute | solution.py:87
  38.8 0.1 constant_dynamic-slice_fusion
  38.9 0.1 reshape.121
  39.0 0.1 fusion.20
  39.2 3.4 %fusion.21 = f32[3,1024,16,3]{1,2,3,0:T(8,128)S(1)} fusion(bf16[3,640,1024,1]{1,2,3,0:T(8,128)(2,1)} %bitcast.40, bf16[16,3,3,640]{3,0,2,1:T(8,128)(2,1)S(1)} %copy_dynamic-update-slice_fusion), kind=kOutput, calls=%fused_computation.69 | convolution fusion | flops 188743680 | bytes 4706304 | tf_op jit(solution)/shard_map/while/body/eval_jaxpr/scbj,cjq->scbq/dot_general | solution.py:105
  42.6 0.1 copy.47
  42.7 0.4 convolution_multiply_fusion.1
  43.0 0.3 fusion.3
  43.3 0.2 fusion.4
  43.5 0.1 copy.29
  43.6 0.1 div.31
  43.8 0.1 slice_select_fusion.5
  43.9 0.1 slice_select_fusion.4
  44.0 0.1 slice_select_fusion.3
  44.2 0.1 slice_select_fusion.2
  44.3 0.1 slice_select_fusion.1
  44.5 0.1 slice_select_fusion
  44.6 0.1 fusion.19
  44.7 0.7 %fusion.14 = f32[8,256]{1,0:T(8,128)} fusion(f32[8,16,257]{2,1,0:T(8,128)S(1)} %get-tuple-element.20, f32[8,16,257]{2,1,0:T(8,128)S(1)} %get-tuple-element.19, f32[8,16]{1,0:T(8,128)S(1)} %convert_element_type.24, pred[8,16]{1,0:T(8,128)(4,1)S(1)} %get-tuple-element.35), kind=kLoop, calls=%fused_computation.25 | loop fusion | flops 96256 | bytes 270976 | tf_op jit(solution)/shard_map/while/body/eval_jaxpr/reduce_sum | solution.py:72
  (25 shorter events, 0.4 us)
Async XLA Ops:
  0.0 25.6 %collective-permute-start = (bf16[1,3,896]{2,1,0:T(4,128)(2,1)}, bf16[1,3,896]{2,1,0:T(4,128)(2,1)S(1)}, u32[]{:S(2)}, u32[]{:S(2)}) collective-permute-start(bf16[1,3,896]{2,1,0:T(4,128)(2,1)} %param.5), channel_id=1, source_target_pairs={{0,15},{1,0},{2,1},{3,2},{4,3},{5,4},{6,5},{7,6},{8,7},{9,8},{10,9... | collective-permute-start | bytes 16136 | tf_op jit(solution)/shard_map/ppermute | solution.py:87
  20.9 2.1 %slice-start = ((bf16[8,3,82048]{2,0,1:T(8,128)(2,1)}), bf16[8,3,81920]{2,0,1:T(8,128)(2,1)S(1)}, s32[]{:S(2)}) async-start(bf16[8,3,82048]{2,0,1:T(8,128)(2,1)} %tile.10), calls=%async_computation | async-start | bytes 7864320 | tf_op jit(solution)/shard_map/slice | solution.py:97
  23.0 2.6 %copy-start = (bf16[1,3,896]{2,1,0:T(4,128)(2,1)S(1)}, bf16[1,3,896]{2,1,0:T(4,128)(2,1)}, u32[]{:S(2)}) copy-start(bf16[1,3,896]{2,1,0:T(4,128)(2,1)} %param.5) | copy-start | bytes 16132
  25.6 3.8 %collective-permute-start.1 = (bf16[2,3,896]{2,1,0:T(4,128)(2,1)S(1)}, bf16[2,3,896]{2,1,0:T(4,128)(2,1)S(1)}, u32[]{:S(2)}, u32[]{:S(2)}) collective-permute-start(bf16[2,3,896]{2,1,0:T(4,128)(2,1)S(1)} %pad_maximum_fusion.2), channel_id=1, source_target_pairs={{0,14},{1,15},{2,0},{3,1},{4,2},{5,3},{6,4},{7,5},{8,6},{9,7},{10,... | collective-permute-start | bytes 32264 | tf_op jit(solution)/shard_map/ppermute | solution.py:87
  29.4 3.9 %collective-permute-start.2 = (bf16[4,3,896]{2,1,0:T(4,128)(2,1)S(1)}, bf16[4,3,896]{2,1,0:T(4,128)(2,1)S(1)}, u32[]{:S(2)}, u32[]{:S(2)}) collective-permute-start(bf16[4,3,896]{2,1,0:T(4,128)(2,1)S(1)} %pad_maximum_fusion.1), channel_id=1, source_target_pairs={{0,12},{1,13},{2,14},{3,15},{4,0},{5,1},{6,2},{7,3},{8,4},{9,5},{1... | collective-permute-start | bytes 64520 | tf_op jit(solution)/shard_map/ppermute | solution.py:87
  33.4 5.3 %collective-permute-start.3 = (bf16[8,3,896]{2,1,0:T(4,128)(2,1)S(1)}, bf16[8,3,896]{2,1,0:T(4,128)(2,1)S(1)}, u32[]{:S(2)}, u32[]{:S(2)}) collective-permute-start(bf16[8,3,896]{2,1,0:T(4,128)(2,1)S(1)} %pad_maximum_fusion), channel_id=1, source_target_pairs={{0,8},{1,9},{2,10},{3,11},{4,12},{5,13},{6,14},{7,15},{8,0},{9,1},... | collective-permute-start | bytes 129032 | tf_op jit(solution)/shard_map/ppermute | solution.py:87
